TPU v7x, 128 devices: a whole 4x4x4 slice. The times are simulated.
128 devices in a mesh: grp: 8 (over y, core), leaf: 16 (over x, z).
Axes of the slice: x: 4, y: 4, z: 4, core: 2. Of those that a mesh axis runs over, the one named last changes fastest.
Arguments:
- points: bfloat16 [32, 262144], P(None, ('grp', 'leaf')), may hold values from -6 to 6
- right_side: float32 [8, 262144], P(None, ('grp', 'leaf')), may hold values from -6 to 6
- neighbours: int32 [256, 8], P(('grp', 'leaf')), may hold values from 0 to 31, as said below
- neighbour_count: int32 [256], P(('grp', 'leaf')), may hold values from 1 to 8, as said below
- mid_skeleton: int32 [128, 256], P(('grp', 'leaf')), may hold values from 0 to 2047, as said below
- top_skeleton: int32 [8, 256], P('grp'), may hold values from 0 to 32767, as said below
- mid_basis: float32 [256, 262144], P(None, ('grp', 'leaf')), may hold values from -0.125 to 0.125
- top_basis: float32 [256, 262144], P(None, ('grp', 'leaf')), may hold values from -0.125 to 0.125
- noise_level: float32 [1], replicated, may hold values from 1 to 2
Outputs:
- solution: float32 [8, 262144], P(None, ('grp', 'leaf'))
- residual: float32 [8, 262144], P(None, ('grp', 'leaf'))
Inputs may be any that keep to these rules, and one draw needn't show every extreme that they name: `neighbours`: entry 0 of leaf l is l itself; entries 1 to neighbour_count[l] - 1 are distinct other leaves of the same subtree; later entries repeat l. Leaf j is listed by l exactly when l is listed by j. `neighbour_count`: the number of listed entries of each leaf, itself included. `mid_skeleton`: distinct positions within each block. `top_skeleton`: distinct positions within each subtree.
All inputs are finite; a program needn't handle non-finite values.
Results may differ from a plain program's by a relative error of at most 0.0003.
Values may be sent and summed in bfloat16 or wider, within the bound.
A program may use at most 128 MiB of HBM per device.

v0:
```python
import jax
import jax.numpy as jnp
from jax import lax
from jax.sharding import PartitionSpec as P

FEATURES = 32
LEAF = 1024
RANK = 256
NEIGHBOURS = 8
ITERS = 2


def exact_dot(left_cols, right_cols):
    return jnp.dot(
        left_cols, right_cols, precision=lax.Precision.HIGHEST, preferred_element_type=jnp.float32
    )


def transposed_dot(left_cols, right_cols):
    return lax.dot_general(
        left_cols,
        right_cols,
        (((1,), (1,)), ((), ())),
        precision=lax.Precision.HIGHEST,
        preferred_element_type=jnp.float32,
    )


def kernel(left_cols, right_cols):
    cross_terms = lax.dot_general(
        left_cols, right_cols, (((0,), (0,)), ((), ())), preferred_element_type=jnp.float32
    )
    left_sq = jnp.sum(jnp.square(left_cols.astype(jnp.float32)), axis=0)
    right_sq = jnp.sum(jnp.square(right_cols.astype(jnp.float32)), axis=0)
    return jnp.exp((2.0 * cross_terms - left_sq[:, None] - right_sq[None, :]) / FEATURES)


def residual_norm(residual):
    return lax.psum(jnp.sum(residual * residual, axis=1), ("grp", "leaf"))


def on_device(
    points,
    right_side,
    neighbours,
    neighbour_count,
    mid_skeleton,
    top_skeleton,
    mid_basis,
    top_basis,
    noise_level,
):
    leaf_span = points.shape[1] // LEAF
    own_mid = jnp.take(points, mid_skeleton[0], axis=1)
    group_points, mid_points = (
        lax.all_gather(points, "leaf", axis=1, tiled=True),
        lax.all_gather(own_mid, "leaf", axis=1, tiled=True),
    )
    own_root = jnp.take(group_points, top_skeleton[0], axis=1)
    root_points = lax.all_gather(own_root, "grp", axis=1, tiled=True)
    mid_kernel = kernel(mid_points, own_mid)
    root_kernel = kernel(root_points, own_root)
    self_kernels = [
        kernel(
            points[:, leaf_slot * LEAF : (leaf_slot + 1) * LEAF],
            points[:, leaf_slot * LEAF : (leaf_slot + 1) * LEAF],
        )
        for leaf_slot in range(leaf_span)
    ]

    def near_rows(vector, group_vector):
        pieces = []
        for leaf_slot in range(leaf_span):
            own_points = points[:, leaf_slot * LEAF : (leaf_slot + 1) * LEAF]
            own_vector = vector[:, leaf_slot * LEAF : (leaf_slot + 1) * LEAF]
            listed = neighbour_count[leaf_slot]
            running = listed.astype(jnp.float32) * exact_dot(own_vector, self_kernels[leaf_slot])

            def slot_step(
                slot_index, carried, leaf_slot=leaf_slot, own_points=own_points, listed=listed
            ):
                partner = neighbours[leaf_slot, slot_index]

                def compute(current):
                    partner_points = lax.dynamic_slice_in_dim(group_points, partner * LEAF, LEAF, 1)
                    partner_vector = lax.dynamic_slice_in_dim(group_vector, partner * LEAF, LEAF, 1)
                    return current + exact_dot(partner_vector, kernel(partner_points, own_points))

                return lax.cond(slot_index < listed, compute, lambda current: current, carried)

            running = lax.fori_loop(1, NEIGHBOURS, slot_step, running)
            pieces.append(running)
        return jnp.concatenate(pieces, axis=1)

    solution = jnp.zeros_like(right_side)
    residual = right_side
    direction = right_side
    norm_now = residual_norm(residual)
    for step_index in range(ITERS):
        mid_part = transposed_dot(direction, mid_basis)
        top_part = transposed_dot(direction, top_basis)
        operate_group_vector = lax.all_gather(direction, "leaf", axis=1, tiled=True)
        mid_weights = lax.all_gather(mid_part, "leaf", axis=1, tiled=True)
        summed = lax.psum(top_part, "leaf")
        top_weights = lax.all_gather(summed, "grp", axis=1, tiled=True)
        near_term = near_rows(direction, operate_group_vector)
        near_term = LEAF ** (-0.5) * near_term
        mid_image = RANK ** (-0.5) * exact_dot(mid_weights, mid_kernel)
        mid_term = exact_dot(mid_image, mid_basis)
        top_image = RANK ** (-0.5) * exact_dot(top_weights, root_kernel)
        top_term = exact_dot(top_image, top_basis)
        image = noise_level[0] * direction + near_term + mid_term + top_term
        step_size = norm_now / lax.psum(jnp.sum(direction * image, axis=1), ("grp", "leaf"))
        solution = solution + step_size[:, None] * direction
        residual = residual - step_size[:, None] * image
        if step_index + 1 < ITERS:
            norm_next = residual_norm(residual)
            direction = residual + (norm_next / norm_now)[:, None] * direction
            norm_now = norm_next
    return (solution, residual)


def solution(mesh):
    placed = (
        P(None, ("grp", "leaf")),
        P(None, ("grp", "leaf")),
        P(("grp", "leaf"), None),
        P(("grp", "leaf")),
        P(("grp", "leaf"), None),
        P("grp", None),
        P(None, ("grp", "leaf")),
        P(None, ("grp", "leaf")),
        P(),
    )
    return jax.shard_map(
        on_device,
        mesh=mesh,
        in_specs=placed,
        out_specs=(P(None, ("grp", "leaf")), P(None, ("grp", "leaf"))),
        check_vma=False,
    )
```

profile of v0, /device:TPU:1, one launch (start us, length us, event | category | flops | bytes accessed | tf_op | source)
XLA Modules:
  0.0 725.7 jit_solution(11971487145099830624)
XLA Ops:
  26.1 36.6 %psum.43 = f32[8,256]{1,0:T(8,128)S(1)} all-reduce(f32[8,256]{1,0:T(8,128)S(1)} %fusion.145), channel_id=1, replica_groups=mesh['grp'=8,'leaf'=16] {'leaf'}, use_global_device_ids=true, to_apply=%region_18.19 | all-reduce | flops 2048 | bytes 16384 | tf_op jit(solution)/shard_map/psum | solution.py:104
  62.7 21.0 %all_gather.31 = f32[8,2048]{1,0:T(8,128)S(1)} all-gather(f32[8,256]{1,0:T(8,128)S(1)} %psum.43), channel_id=1, replica_groups=mesh['grp'=8,'leaf'=16] {'grp'}, dimensions={1}, use_global_device_ids=true | all-gather | bytes 73728 | tf_op jit(solution)/shard_map/all_gather | solution.py:105
  83.7 15.4 %all_gather.29 = f32[8,4096]{1,0:T(8,128)S(1)} all-gather(f32[8,256]{1,0:T(8,128)S(1)} %fusion.144), channel_id=1, replica_groups=mesh['grp'=8,'leaf'=16] {'leaf'}, dimensions={1}, use_global_device_ids=true | all-gather | bytes 139264 | tf_op jit(solution)/shard_map/all_gather | solution.py:103
  101.1 20.8 %all_gather.30 = bf16[32,4096]{0,1:T(8,128)(2,1)S(1)} all-gather(bf16[32,256]{0,1:T(8,128)(2,1)S(1)} %get-tuple-element.873), channel_id=1, replica_groups=mesh['grp'=8,'leaf'=16] {'leaf'}, dimensions={1}, use_global_device_ids=true | all-gather | bytes 278528 | tf_op jit(solution)/shard_map/all_gather | solution.py:57
  132.0 7.9 %copy.18 = bf16[32,32768]{1,0:T(8,128)(2,1)} copy(bf16[32,32768]{0,1:T(8,128)(2,1)} %all-gather.6.cloned.1.call-done) | data formatting | bytes 4194304 | tf_op jit(solution)/shard_map/while | solution.py:91
  139.9 5.2 gather_fusion.1
  145.3 23.1 %all_gather.32 = bf16[32,2048]{0,1:T(8,128)(2,1)S(1)} all-gather(bf16[32,256]{0,1:T(8,128)(2,1)S(1)} %get-tuple-element.871), channel_id=1, replica_groups=mesh['grp'=8,'leaf'=16] {'grp'}, dimensions={1}, use_global_device_ids=true | all-gather | bytes 147456 | tf_op jit(solution)/shard_map/all_gather | solution.py:60
  168.8 64.4 %while.65 = (s32[]{:T(128)}, f32[8,1024]{1,0:T(8,128)S(1)}, s32[]{:T(128)}, s32[2,8]{1,0:T(2,128)S(1)}, f32[8,32768]{1,0:T(8,128)}, /*index=5*/bf16[32,32768]{1,0:T(8,128)(2,1)}, bf16[32,1024]{1,0:T(8,128)(2,1)S(1)}, s32[]{:T(128)}) while((s32[]{:T(128)}, f32[8,1024]{1,0:T(8,128)S(1)}, s32[]{:T(128)}, s32[2,8]{1,0:T(2,128)S(1)}, ...), condition=%wide.region_15.16_spmd, body=%wide.region_10.15_spmd.sunk | while | flops 172169216 | bytes 8765687 | solution.py:91
  169.7 8.5 %conditional.9 = (f32[8,1024]{1,0:T(8,128)S(1)}) conditional(s32[]{:T(128)} %convert_element_type.119, f32[8,1024]{1,0:T(8,128)S(1)} %get-tuple-element.1072, (s32[]{:T(128)}, s32[2,8]{1,0:T(2,128)S(1)}, f32[8,32768]{1,0:T(8,128)}, bf16[32,32768]{1,0:T(8,128)(2,1)}, bf16[32,1024]{1,0:T(8,128)(2,1)S(1)}, /*index=5*/f32[8,1024]{1,0:T(8,128)S(1)}) %tuple.187), branch_computations={%region_11.11_spmd, %region_12.14_spmd} | conditional | flops 172169216 | bytes 8765540 | solution.py:89
  178.9 8.5 %conditional.9 = (f32[8,1024]{1,0:T(8,128)S(1)}) conditional(s32[]{:T(128)} %convert_element_type.119, f32[8,1024]{1,0:T(8,128)S(1)} %get-tuple-element.1072, (s32[]{:T(128)}, s32[2,8]{1,0:T(2,128)S(1)}, f32[8,32768]{1,0:T(8,128)}, bf16[32,32768]{1,0:T(8,128)(2,1)}, bf16[32,1024]{1,0:T(8,128)(2,1)S(1)}, /*index=5*/f32[8,1024]{1,0:T(8,128)S(1)}) %tuple.187), branch_computations={%region_11.11_spmd, %region_12.14_spmd} | conditional | flops 172169216 | bytes 8765540 | solution.py:89
  188.0 8.5 %conditional.9 = (f32[8,1024]{1,0:T(8,128)S(1)}) conditional(s32[]{:T(128)} %convert_element_type.119, f32[8,1024]{1,0:T(8,128)S(1)} %get-tuple-element.1072, (s32[]{:T(128)}, s32[2,8]{1,0:T(2,128)S(1)}, f32[8,32768]{1,0:T(8,128)}, bf16[32,32768]{1,0:T(8,128)(2,1)}, bf16[32,1024]{1,0:T(8,128)(2,1)S(1)}, /*index=5*/f32[8,1024]{1,0:T(8,128)S(1)}) %tuple.187), branch_computations={%region_11.11_spmd, %region_12.14_spmd} | conditional | flops 172169216 | bytes 8765540 | solution.py:89
  197.2 8.5 %conditional.9 = (f32[8,1024]{1,0:T(8,128)S(1)}) conditional(s32[]{:T(128)} %convert_element_type.119, f32[8,1024]{1,0:T(8,128)S(1)} %get-tuple-element.1072, (s32[]{:T(128)}, s32[2,8]{1,0:T(2,128)S(1)}, f32[8,32768]{1,0:T(8,128)}, bf16[32,32768]{1,0:T(8,128)(2,1)}, bf16[32,1024]{1,0:T(8,128)(2,1)S(1)}, /*index=5*/f32[8,1024]{1,0:T(8,128)S(1)}) %tuple.187), branch_computations={%region_11.11_spmd, %region_12.14_spmd} | conditional | flops 172169216 | bytes 8765540 | solution.py:89
  206.4 8.5 %conditional.9 = (f32[8,1024]{1,0:T(8,128)S(1)}) conditional(s32[]{:T(128)} %convert_element_type.119, f32[8,1024]{1,0:T(8,128)S(1)} %get-tuple-element.1072, (s32[]{:T(128)}, s32[2,8]{1,0:T(2,128)S(1)}, f32[8,32768]{1,0:T(8,128)}, bf16[32,32768]{1,0:T(8,128)(2,1)}, bf16[32,1024]{1,0:T(8,128)(2,1)S(1)}, /*index=5*/f32[8,1024]{1,0:T(8,128)S(1)}) %tuple.187), branch_computations={%region_11.11_spmd, %region_12.14_spmd} | conditional | flops 172169216 | bytes 8765540 | solution.py:89
  215.6 8.5 %conditional.9 = (f32[8,1024]{1,0:T(8,128)S(1)}) conditional(s32[]{:T(128)} %convert_element_type.119, f32[8,1024]{1,0:T(8,128)S(1)} %get-tuple-element.1072, (s32[]{:T(128)}, s32[2,8]{1,0:T(2,128)S(1)}, f32[8,32768]{1,0:T(8,128)}, bf16[32,32768]{1,0:T(8,128)(2,1)}, bf16[32,1024]{1,0:T(8,128)(2,1)S(1)}, /*index=5*/f32[8,1024]{1,0:T(8,128)S(1)}) %tuple.187), branch_computations={%region_11.11_spmd, %region_12.14_spmd} | conditional | flops 172169216 | bytes 8765540 | solution.py:89
  224.7 8.5 %conditional.9 = (f32[8,1024]{1,0:T(8,128)S(1)}) conditional(s32[]{:T(128)} %convert_element_type.119, f32[8,1024]{1,0:T(8,128)S(1)} %get-tuple-element.1072, (s32[]{:T(128)}, s32[2,8]{1,0:T(2,128)S(1)}, f32[8,32768]{1,0:T(8,128)}, bf16[32,32768]{1,0:T(8,128)(2,1)}, bf16[32,1024]{1,0:T(8,128)(2,1)S(1)}, /*index=5*/f32[8,1024]{1,0:T(8,128)S(1)}) %tuple.187), branch_computations={%region_11.11_spmd, %region_12.14_spmd} | conditional | flops 172169216 | bytes 8765540 | solution.py:89
  233.2 67.7 %while.64 = (s32[]{:T(128)}, f32[8,1024]{1,0:T(8,128)S(1)}, s32[]{:T(128)}, s32[2,8]{1,0:T(2,128)S(1)}, f32[8,32768]{1,0:T(8,128)}, /*index=5*/bf16[32,32768]{1,0:T(8,128)(2,1)}, bf16[32,1024]{1,0:T(8,128)(2,1)S(1)}, s32[]{:T(128)}) while((s32[]{:T(128)}, f32[8,1024]{1,0:T(8,128)S(1)}, s32[]{:T(128)}, s32[2,8]{1,0:T(2,128)S(1)}, ...), condition=%wide.region_8.9_spmd, body=%wide.region_3.8_spmd.sunk | while | flops 172169216 | bytes 8765687 | solution.py:91
  233.9 9.0 %conditional.8 = (f32[8,1024]{1,0:T(8,128)S(1)}) conditional(s32[]{:T(128)} %convert_element_type.118, f32[8,1024]{1,0:T(8,128)S(1)} %get-tuple-element.1096, (s32[]{:T(128)}, s32[2,8]{1,0:T(2,128)S(1)}, f32[8,32768]{1,0:T(8,128)}, bf16[32,32768]{1,0:T(8,128)(2,1)}, bf16[32,1024]{1,0:T(8,128)(2,1)S(1)}, /*index=5*/f32[8,1024]{1,0:T(8,128)S(1)}) %tuple.185), branch_computations={%region_4.4_spmd, %region_5.7_spmd} | conditional | flops 172169216 | bytes 8765540 | solution.py:89
  243.6 9.0 %conditional.8 = (f32[8,1024]{1,0:T(8,128)S(1)}) conditional(s32[]{:T(128)} %convert_element_type.118, f32[8,1024]{1,0:T(8,128)S(1)} %get-tuple-element.1096, (s32[]{:T(128)}, s32[2,8]{1,0:T(2,128)S(1)}, f32[8,32768]{1,0:T(8,128)}, bf16[32,32768]{1,0:T(8,128)(2,1)}, bf16[32,1024]{1,0:T(8,128)(2,1)S(1)}, /*index=5*/f32[8,1024]{1,0:T(8,128)S(1)}) %tuple.185), branch_computations={%region_4.4_spmd, %region_5.7_spmd} | conditional | flops 172169216 | bytes 8765540 | solution.py:89
  253.2 9.0 %conditional.8 = (f32[8,1024]{1,0:T(8,128)S(1)}) conditional(s32[]{:T(128)} %convert_element_type.118, f32[8,1024]{1,0:T(8,128)S(1)} %get-tuple-element.1096, (s32[]{:T(128)}, s32[2,8]{1,0:T(2,128)S(1)}, f32[8,32768]{1,0:T(8,128)}, bf16[32,32768]{1,0:T(8,128)(2,1)}, bf16[32,1024]{1,0:T(8,128)(2,1)S(1)}, /*index=5*/f32[8,1024]{1,0:T(8,128)S(1)}) %tuple.185), branch_computations={%region_4.4_spmd, %region_5.7_spmd} | conditional | flops 172169216 | bytes 8765540 | solution.py:89
  262.9 9.0 %conditional.8 = (f32[8,1024]{1,0:T(8,128)S(1)}) conditional(s32[]{:T(128)} %convert_element_type.118, f32[8,1024]{1,0:T(8,128)S(1)} %get-tuple-element.1096, (s32[]{:T(128)}, s32[2,8]{1,0:T(2,128)S(1)}, f32[8,32768]{1,0:T(8,128)}, bf16[32,32768]{1,0:T(8,128)(2,1)}, bf16[32,1024]{1,0:T(8,128)(2,1)S(1)}, /*index=5*/f32[8,1024]{1,0:T(8,128)S(1)}) %tuple.185), branch_computations={%region_4.4_spmd, %region_5.7_spmd} | conditional | flops 172169216 | bytes 8765540 | solution.py:89
  272.6 9.0 %conditional.8 = (f32[8,1024]{1,0:T(8,128)S(1)}) conditional(s32[]{:T(128)} %convert_element_type.118, f32[8,1024]{1,0:T(8,128)S(1)} %get-tuple-element.1096, (s32[]{:T(128)}, s32[2,8]{1,0:T(2,128)S(1)}, f32[8,32768]{1,0:T(8,128)}, bf16[32,32768]{1,0:T(8,128)(2,1)}, bf16[32,1024]{1,0:T(8,128)(2,1)S(1)}, /*index=5*/f32[8,1024]{1,0:T(8,128)S(1)}) %tuple.185), branch_computations={%region_4.4_spmd, %region_5.7_spmd} | conditional | flops 172169216 | bytes 8765540 | solution.py:89
  282.2 9.0 %conditional.8 = (f32[8,1024]{1,0:T(8,128)S(1)}) conditional(s32[]{:T(128)} %convert_element_type.118, f32[8,1024]{1,0:T(8,128)S(1)} %get-tuple-element.1096, (s32[]{:T(128)}, s32[2,8]{1,0:T(2,128)S(1)}, f32[8,32768]{1,0:T(8,128)}, bf16[32,32768]{1,0:T(8,128)(2,1)}, bf16[32,1024]{1,0:T(8,128)(2,1)S(1)}, /*index=5*/f32[8,1024]{1,0:T(8,128)S(1)}) %tuple.185), branch_computations={%region_4.4_spmd, %region_5.7_spmd} | conditional | flops 172169216 | bytes 8765540 | solution.py:89
  291.9 9.0 %conditional.8 = (f32[8,1024]{1,0:T(8,128)S(1)}) conditional(s32[]{:T(128)} %convert_element_type.118, f32[8,1024]{1,0:T(8,128)S(1)} %get-tuple-element.1096, (s32[]{:T(128)}, s32[2,8]{1,0:T(2,128)S(1)}, f32[8,32768]{1,0:T(8,128)}, bf16[32,32768]{1,0:T(8,128)(2,1)}, bf16[32,1024]{1,0:T(8,128)(2,1)S(1)}, /*index=5*/f32[8,1024]{1,0:T(8,128)S(1)}) %tuple.185), branch_computations={%region_4.4_spmd, %region_5.7_spmd} | conditional | flops 172169216 | bytes 8765540 | solution.py:89
  304.9 62.4 %all-reduce = (f32[8]{0:T(128)S(1)}, f32[8]{0:T(128)S(1)}) all-reduce(f32[8]{0:T(128)S(1)} %get-tuple-element.811, f32[8]{0:T(128)S(1)} %get-tuple-element.810), channel_id=1, replica_groups=mesh['grp'=8,'leaf'=16] {'grp','leaf'}, use_global_device_ids=true, to_apply=%region_1.2 | all-reduce | flops 16 | bytes 128 | tf_op jit(solution)/shard_map/psum | solution.py:39
  367.5 64.1 %psum.45 = f32[8]{0:T(128)S(1)} all-reduce(f32[8]{0:T(128)S(1)} %multiply_reduce_fusion.15), channel_id=1, replica_groups=mesh['grp'=8,'leaf'=16] {'grp','leaf'}, use_global_device_ids=true, to_apply=%region_24.25 | all-reduce | flops 8 | bytes 64 | tf_op jit(solution)/shard_map/psum | solution.py:39
  434.9 31.8 %psum.46 = f32[8,256]{1,0:T(8,128)S(1)} all-reduce(f32[8,256]{1,0:T(8,128)S(1)} %fusion.147), channel_id=1, replica_groups=mesh['grp'=8,'leaf'=16] {'leaf'}, use_global_device_ids=true, to_apply=%region_37.38 | all-reduce | flops 2048 | bytes 16384 | tf_op jit(solution)/shard_map/psum | solution.py:104
  466.8 20.3 %all_gather.35 = f32[8,2048]{1,0:T(8,128)S(1)} all-gather(f32[8,256]{1,0:T(8,128)S(1)} %psum.46), channel_id=1, replica_groups=mesh['grp'=8,'leaf'=16] {'grp'}, dimensions={1}, use_global_device_ids=true | all-gather | bytes 73728 | tf_op jit(solution)/shard_map/all_gather | solution.py:105
  490.6 15.6 %all_gather.34 = f32[8,4096]{1,0:T(8,128)S(1)} all-gather(f32[8,256]{1,0:T(8,128)S(1)} %fusion.146), channel_id=1, replica_groups=mesh['grp'=8,'leaf'=16] {'leaf'}, dimensions={1}, use_global_device_ids=true | all-gather | bytes 139264 | tf_op jit(solution)/shard_map/all_gather | solution.py:103
  516.4 64.7 %while.67 = (s32[]{:T(128)}, f32[8,1024]{1,0:T(8,128)S(1)}, s32[]{:T(128)}, s32[2,8]{1,0:T(2,128)S(1)}, f32[8,32768]{1,0:T(8,128)}, /*index=5*/bf16[32,32768]{1,0:T(8,128)(2,1)}, bf16[32,1024]{1,0:T(8,128)(2,1)S(1)}, s32[]{:T(128)}) while((s32[]{:T(128)}, f32[8,1024]{1,0:T(8,128)S(1)}, s32[]{:T(128)}, s32[2,8]{1,0:T(2,128)S(1)}, ...), condition=%wide.region_36.37_spmd, body=%wide.region_31.36_spmd.sunk | while | flops 172169216 | bytes 8765687 | solution.py:91
  517.3 8.5 %conditional.11 = (f32[8,1024]{1,0:T(8,128)S(1)}) conditional(s32[]{:T(128)} %convert_element_type.121, f32[8,1024]{1,0:T(8,128)S(1)} %get-tuple-element.1120, (s32[]{:T(128)}, s32[2,8]{1,0:T(2,128)S(1)}, f32[8,32768]{1,0:T(8,128)}, bf16[32,32768]{1,0:T(8,128)(2,1)}, bf16[32,1024]{1,0:T(8,128)(2,1)S(1)}, /*index=5*/f32[8,1024]{1,0:T(8,128)S(1)}) %tuple.191), branch_computations={%region_32.32_spmd, %region_33.0_spmd} | conditional | flops 172169216 | bytes 8765540 | solution.py:89
  526.5 8.5 %conditional.11 = (f32[8,1024]{1,0:T(8,128)S(1)}) conditional(s32[]{:T(128)} %convert_element_type.121, f32[8,1024]{1,0:T(8,128)S(1)} %get-tuple-element.1120, (s32[]{:T(128)}, s32[2,8]{1,0:T(2,128)S(1)}, f32[8,32768]{1,0:T(8,128)}, bf16[32,32768]{1,0:T(8,128)(2,1)}, bf16[32,1024]{1,0:T(8,128)(2,1)S(1)}, /*index=5*/f32[8,1024]{1,0:T(8,128)S(1)}) %tuple.191), branch_computations={%region_32.32_spmd, %region_33.0_spmd} | conditional | flops 172169216 | bytes 8765540 | solution.py:89
  535.7 8.5 %conditional.11 = (f32[8,1024]{1,0:T(8,128)S(1)}) conditional(s32[]{:T(128)} %convert_element_type.121, f32[8,1024]{1,0:T(8,128)S(1)} %get-tuple-element.1120, (s32[]{:T(128)}, s32[2,8]{1,0:T(2,128)S(1)}, f32[8,32768]{1,0:T(8,128)}, bf16[32,32768]{1,0:T(8,128)(2,1)}, bf16[32,1024]{1,0:T(8,128)(2,1)S(1)}, /*index=5*/f32[8,1024]{1,0:T(8,128)S(1)}) %tuple.191), branch_computations={%region_32.32_spmd, %region_33.0_spmd} | conditional | flops 172169216 | bytes 8765540 | solution.py:89
  544.9 8.5 %conditional.11 = (f32[8,1024]{1,0:T(8,128)S(1)}) conditional(s32[]{:T(128)} %convert_element_type.121, f32[8,1024]{1,0:T(8,128)S(1)} %get-tuple-element.1120, (s32[]{:T(128)}, s32[2,8]{1,0:T(2,128)S(1)}, f32[8,32768]{1,0:T(8,128)}, bf16[32,32768]{1,0:T(8,128)(2,1)}, bf16[32,1024]{1,0:T(8,128)(2,1)S(1)}, /*index=5*/f32[8,1024]{1,0:T(8,128)S(1)}) %tuple.191), branch_computations={%region_32.32_spmd, %region_33.0_spmd} | conditional | flops 172169216 | bytes 8765540 | solution.py:89
  554.1 8.5 %conditional.11 = (f32[8,1024]{1,0:T(8,128)S(1)}) conditional(s32[]{:T(128)} %convert_element_type.121, f32[8,1024]{1,0:T(8,128)S(1)} %get-tuple-element.1120, (s32[]{:T(128)}, s32[2,8]{1,0:T(2,128)S(1)}, f32[8,32768]{1,0:T(8,128)}, bf16[32,32768]{1,0:T(8,128)(2,1)}, bf16[32,1024]{1,0:T(8,128)(2,1)S(1)}, /*index=5*/f32[8,1024]{1,0:T(8,128)S(1)}) %tuple.191), branch_computations={%region_32.32_spmd, %region_33.0_spmd} | conditional | flops 172169216 | bytes 8765540 | solution.py:89
  563.3 8.5 %conditional.11 = (f32[8,1024]{1,0:T(8,128)S(1)}) conditional(s32[]{:T(128)} %convert_element_type.121, f32[8,1024]{1,0:T(8,128)S(1)} %get-tuple-element.1120, (s32[]{:T(128)}, s32[2,8]{1,0:T(2,128)S(1)}, f32[8,32768]{1,0:T(8,128)}, bf16[32,32768]{1,0:T(8,128)(2,1)}, bf16[32,1024]{1,0:T(8,128)(2,1)S(1)}, /*index=5*/f32[8,1024]{1,0:T(8,128)S(1)}) %tuple.191), branch_computations={%region_32.32_spmd, %region_33.0_spmd} | conditional | flops 172169216 | bytes 8765540 | solution.py:89
  572.6 8.5 %conditional.11 = (f32[8,1024]{1,0:T(8,128)S(1)}) conditional(s32[]{:T(128)} %convert_element_type.121, f32[8,1024]{1,0:T(8,128)S(1)} %get-tuple-element.1120, (s32[]{:T(128)}, s32[2,8]{1,0:T(2,128)S(1)}, f32[8,32768]{1,0:T(8,128)}, bf16[32,32768]{1,0:T(8,128)(2,1)}, bf16[32,1024]{1,0:T(8,128)(2,1)S(1)}, /*index=5*/f32[8,1024]{1,0:T(8,128)S(1)}) %tuple.191), branch_computations={%region_32.32_spmd, %region_33.0_spmd} | conditional | flops 172169216 | bytes 8765540 | solution.py:89
  581.1 66.2 %while.66 = (s32[]{:T(128)}, f32[8,1024]{1,0:T(8,128)S(1)}, s32[]{:T(128)}, s32[2,8]{1,0:T(2,128)S(1)}, f32[8,32768]{1,0:T(8,128)}, /*index=5*/bf16[32,32768]{1,0:T(8,128)(2,1)}, bf16[32,1024]{1,0:T(8,128)(2,1)S(1)}, s32[]{:T(128)}) while((s32[]{:T(128)}, f32[8,1024]{1,0:T(8,128)S(1)}, s32[]{:T(128)}, s32[2,8]{1,0:T(2,128)S(1)}, ...), condition=%wide.region_30.31_spmd, body=%wide.region_25.30_spmd.sunk | while | flops 172169216 | bytes 8765687 | solution.py:91
  581.8 8.8 %conditional.10 = (f32[8,1024]{1,0:T(8,128)S(1)}) conditional(s32[]{:T(128)} %convert_element_type.120, f32[8,1024]{1,0:T(8,128)S(1)} %get-tuple-element.1144, (s32[]{:T(128)}, s32[2,8]{1,0:T(2,128)S(1)}, f32[8,32768]{1,0:T(8,128)}, bf16[32,32768]{1,0:T(8,128)(2,1)}, bf16[32,1024]{1,0:T(8,128)(2,1)S(1)}, /*index=5*/f32[8,1024]{1,0:T(8,128)S(1)}) %tuple.189), branch_computations={%region_26.26_spmd, %region_27.29_spmd} | conditional | flops 172169216 | bytes 8765540 | solution.py:89
  586.8 3.7 fusion.50
  591.3 8.8 %conditional.10 = (f32[8,1024]{1,0:T(8,128)S(1)}) conditional(s32[]{:T(128)} %convert_element_type.120, f32[8,1024]{1,0:T(8,128)S(1)} %get-tuple-element.1144, (s32[]{:T(128)}, s32[2,8]{1,0:T(2,128)S(1)}, f32[8,32768]{1,0:T(8,128)}, bf16[32,32768]{1,0:T(8,128)(2,1)}, bf16[32,1024]{1,0:T(8,128)(2,1)S(1)}, /*index=5*/f32[8,1024]{1,0:T(8,128)S(1)}) %tuple.189), branch_computations={%region_26.26_spmd, %region_27.29_spmd} | conditional | flops 172169216 | bytes 8765540 | solution.py:89
  596.3 3.7 fusion.50
  600.7 8.8 %conditional.10 = (f32[8,1024]{1,0:T(8,128)S(1)}) conditional(s32[]{:T(128)} %convert_element_type.120, f32[8,1024]{1,0:T(8,128)S(1)} %get-tuple-element.1144, (s32[]{:T(128)}, s32[2,8]{1,0:T(2,128)S(1)}, f32[8,32768]{1,0:T(8,128)}, bf16[32,32768]{1,0:T(8,128)(2,1)}, bf16[32,1024]{1,0:T(8,128)(2,1)S(1)}, /*index=5*/f32[8,1024]{1,0:T(8,128)S(1)}) %tuple.189), branch_computations={%region_26.26_spmd, %region_27.29_spmd} | conditional | flops 172169216 | bytes 8765540 | solution.py:89
  605.7 3.7 fusion.50
  610.2 8.8 %conditional.10 = (f32[8,1024]{1,0:T(8,128)S(1)}) conditional(s32[]{:T(128)} %convert_element_type.120, f32[8,1024]{1,0:T(8,128)S(1)} %get-tuple-element.1144, (s32[]{:T(128)}, s32[2,8]{1,0:T(2,128)S(1)}, f32[8,32768]{1,0:T(8,128)}, bf16[32,32768]{1,0:T(8,128)(2,1)}, bf16[32,1024]{1,0:T(8,128)(2,1)S(1)}, /*index=5*/f32[8,1024]{1,0:T(8,128)S(1)}) %tuple.189), branch_computations={%region_26.26_spmd, %region_27.29_spmd} | conditional | flops 172169216 | bytes 8765540 | solution.py:89
  619.6 8.8 %conditional.10 = (f32[8,1024]{1,0:T(8,128)S(1)}) conditional(s32[]{:T(128)} %convert_element_type.120, f32[8,1024]{1,0:T(8,128)S(1)} %get-tuple-element.1144, (s32[]{:T(128)}, s32[2,8]{1,0:T(2,128)S(1)}, f32[8,32768]{1,0:T(8,128)}, bf16[32,32768]{1,0:T(8,128)(2,1)}, bf16[32,1024]{1,0:T(8,128)(2,1)S(1)}, /*index=5*/f32[8,1024]{1,0:T(8,128)S(1)}) %tuple.189), branch_computations={%region_26.26_spmd, %region_27.29_spmd} | conditional | flops 172169216 | bytes 8765540 | solution.py:89
  629.1 8.8 %conditional.10 = (f32[8,1024]{1,0:T(8,128)S(1)}) conditional(s32[]{:T(128)} %convert_element_type.120, f32[8,1024]{1,0:T(8,128)S(1)} %get-tuple-element.1144, (s32[]{:T(128)}, s32[2,8]{1,0:T(2,128)S(1)}, f32[8,32768]{1,0:T(8,128)}, bf16[32,32768]{1,0:T(8,128)(2,1)}, bf16[32,1024]{1,0:T(8,128)(2,1)S(1)}, /*index=5*/f32[8,1024]{1,0:T(8,128)S(1)}) %tuple.189), branch_computations={%region_26.26_spmd, %region_27.29_spmd} | conditional | flops 172169216 | bytes 8765540 | solution.py:89
  638.6 8.8 %conditional.10 = (f32[8,1024]{1,0:T(8,128)S(1)}) conditional(s32[]{:T(128)} %convert_element_type.120, f32[8,1024]{1,0:T(8,128)S(1)} %get-tuple-element.1144, (s32[]{:T(128)}, s32[2,8]{1,0:T(2,128)S(1)}, f32[8,32768]{1,0:T(8,128)}, bf16[32,32768]{1,0:T(8,128)(2,1)}, bf16[32,1024]{1,0:T(8,128)(2,1)S(1)}, /*index=5*/f32[8,1024]{1,0:T(8,128)S(1)}) %tuple.189), branch_computations={%region_26.26_spmd, %region_27.29_spmd} | conditional | flops 172169216 | bytes 8765540 | solution.py:89
  651.2 66.9 %psum.47 = f32[8]{0:T(128)S(1)} all-reduce(f32[8]{0:T(128)S(1)} %get-tuple-element.889), channel_id=1, replica_groups=mesh['grp'=8,'leaf'=16] {'grp','leaf'}, use_global_device_ids=true, to_apply=%region_39.40 | all-reduce | flops 8 | bytes 64 | tf_op jit(solution)/shard_map/psum | solution.py:113
  (191 shorter events, 234.3 us)
Async XLA Ops:
  7.2 17.2 %copy-start = (f32[256,2048]{1,0:T(8,128)S(1)}, f32[256,2048]{1,0:T(8,128)}, u32[]{:S(2)}) copy-start(f32[256,2048]{1,0:T(8,128)} %param.32) | copy-start | bytes 6291460
  7.2 8.4 %copy-start.11 = (bf16[32,2048]{1,0:T(8,128)(2,1)S(1)}, bf16[32,2048]{1,0:T(8,128)(2,1)}, u32[]{:S(2)}) copy-start(bf16[32,2048]{1,0:T(8,128)(2,1)} %param.25) | copy-start | bytes 393220
  7.2 124.8 %all-gather.6.cloned.1.call-start = ((), (), s32[]{:S(2)}) async-start(), calls=%async_computation.1 | async-start | bytes 8912896 | tf_op jit(solution)/shard_map/all_gather | solution.py:56
  9.3 159.5 %all-gather.4.cloned.1.call-start = ((), (), s32[]{:S(2)}) async-start(), calls=%async_computation | async-start | bytes 1114112 | tf_op jit(solution)/shard_map/all_gather | solution.py:102
  10.1 506.3 %all-gather.8.cloned.1.call-start = ((), (), s32[]{:S(2)}) async-start(), calls=%async_computation.2 | async-start | bytes 1114112 | tf_op jit(solution)/shard_map/all_gather | solution.py:102
  11.9 7.0 copy-start.13
  11.9 7.0 copy-start.14
  12.0 7.1 copy-start.12
  12.0 9.1 %copy-start.5 = (f32[8,2048]{1,0:T(8,128)S(1)}, f32[8,2048]{1,0:T(8,128)}, u32[]{:S(2)}) copy-start(f32[8,2048]{1,0:T(8,128)} %param.26) | copy-start | bytes 196612
  122.6 3.0 copy-start.8
  123.8 5.0 copy-start.2
  123.8 5.0 copy-start.6
  132.0 36.8 %copy-start.15 = (s32[2,8]{1,0:T(2,128)S(1)}, s32[2,8]{1,0:T(2,128)}, u32[]{:S(2)}) copy-start(s32[2,8]{1,0:T(2,128)} %param.27) | copy-start | bytes 196
  300.9 1.7 copy-start.1
  301.6 2.0 copy-start.4
  466.8 41.9 %copy-start.3 = (f32[4096,256]{1,0:T(8,128)S(1)}, f32[4096,256]{1,0:T(8,128)}, u32[]{:S(2)}) copy-start(f32[4096,256]{1,0:T(8,128)} %copy-done.2) | copy-start | bytes 12582916
  487.1 23.3 %copy-start.9 = (f32[1024,1024]{1,0:T(8,128)S(1)}, f32[1024,1024]{1,0:T(8,128)}, u32[]{:S(2)}) copy-start(f32[1024,1024]{1,0:T(8,128)} %fusion.132) | copy-start | bytes 12582916
  487.1 23.3 %copy-start.10 = (f32[8,2048]{1,0:T(8,128)S(1)}, f32[8,2048]{1,0:T(8,128)}, u32[]{:S(2)}) copy-start(f32[8,2048]{1,0:T(8,128)} %multiply_add_fusion.1) | copy-start | bytes 196612
  508.7 4.7 copy-start.7
Sparse Core Ops, SparseCore 0:
  10.2 74.7 all-gather.5
  87.1 40.8 all-gather.3
  432.5 37.8 all-gather.7
where the time goes:
time: 737 us; the launch traced here: 726 us
  blocking collectives  378 us (51%)
  matrix products  193 us (26%)
  loops' own time  72.6 us (10%)
  other arithmetic  45.8 us (6%)
  local copies, waits for them, and re-layouts  18.6 us (3%)
  between operations  16.3 us (2%)
    dot_general x40, matrix products, exact_dot(): jnp.dot(left_cols, right_cols, precision=lax.Precision.HIGHEST, preferred...  130 us
    psum x2, blocking collectives, residual_norm(): return lax.psum(jnp.sum(residual * residual, axis=1), ('grp', 'leaf'))  127 us
    psum x2, blocking collectives, on_device(): summed = lax.psum(top_part, 'leaf')  68.4 us
    psum x1, blocking collectives, on_device(): lax.psum(jnp.sum(direction * image, axis=1), ('grp', 'leaf'))  66.9 us
    another operation x28, loops' own time, slot_step(): lax.cond(slot_index < listed, compute, lambda current: current, carried)  52.7 us
    dot_general x32, matrix products, kernel(): lax.dot_general(left_cols, right_cols, (((0,), (0,)), ((), ())), preferre...  52.2 us
    all_gather x2, blocking collectives, on_device(): top_weights = lax.all_gather(summed, 'grp', axis=1, tiled=True)  41.3 us
    all_gather x2, blocking collectives, on_device(): mid_weights = lax.all_gather(mid_part, 'leaf', axis=1, tiled=True)  30.9 us
  transfers between devices with their start and end apart: 3, of which 0 were waited for; matrix products, arithmetic and copies ran while one was open for 8% of the time, Pallas kernels for 0%

commit v1 on v0

v1 whole, which is shorter than its diff:
```python
import math

import jax
import jax.numpy as jnp
from jax import lax
from jax.experimental import pallas as pl
from jax.experimental.pallas import tpu as pltpu
from jax.sharding import PartitionSpec as P

FEATURES = 32
TARGETS = 8
LEAF = 1024
RANK = 256
SLOTS = 8
SIDE = 4
N_LEAF = 16
N_GRP = 8
BLOCK = 2 * LEAF
CHUNK = 512
KEPT = 8
MESH = pl.DeviceIdType.MESH
F32 = jnp.float32
BF16 = jnp.bfloat16
SCALE = math.log2(math.e) / 16.0

LABELS = (
    [(1, 0, None), (3, 0, None), (2, 0, 0), (2, 0, 1)]
    + [(df, ds, None) for df in range(4) for ds in (1, 3)]
    + [(df, 2, part) for df in range(4) for part in (0, 1)]
)
PLACE = {label: i for i, label in enumerate(LABELS)}


def dot(left, right):
    return jnp.dot(left, right, preferred_element_type=F32)


def dot_tn(left, right):
    return lax.dot_general(left, right, (((0,), (0,)), ((), ())), preferred_element_type=F32)


def dot_nt(left, right):
    return lax.dot_general(left, right, (((1,), (1,)), ((), ())), preferred_element_type=F32)


def halves(value):
    high = value.astype(BF16)
    return high, (value - high.astype(F32)).astype(BF16)


def stacked(value):
    high = value.astype(BF16).astype(F32)
    return jnp.concatenate([high, value - high], axis=0).astype(BF16)


def folded(value):
    return value[:TARGETS] + value[TARGETS:]


def thirds(coords):
    scaled = coords.astype(F32) * SCALE
    first = scaled.astype(BF16)
    rest = scaled - first.astype(F32)
    second = rest.astype(BF16)
    third = (rest - second.astype(F32)).astype(BF16)
    return jnp.concatenate([first, second, third], axis=0)


def self_scale(coords):
    wide = coords.astype(F32)
    return jnp.exp2(jnp.sum(wide * wide, axis=0, keepdims=True) * (-0.5 * SCALE))


def kernel_halves(rows, columns3):
    return halves(jnp.exp2(dot_tn(jnp.concatenate([rows, rows, rows], axis=0), columns3)))


def applied(field16, high, low):
    return dot(field16, high) + dot(field16, low)


class Gather:
    def __init__(self, half, me, slot, part, send, recv):
        first, second = lax.div(me, SIDE), lax.rem(me, SIDE)
        if half == 1:
            first, second = second, first
        self.half, self.first, self.second = half, first, second
        self.slot, self.part, self.send, self.recv = slot, part, send, recv
        self.sent = []

    def device(self, df, ds):
        f = lax.rem(self.first + SIDE - df, SIDE)
        s = lax.rem(self.second + SIDE - ds, SIDE)
        return f * SIDE + s if self.half == 0 else s * SIDE + f

    def ref(self, df, ds, part):
        block = self.slot(2 * self.device(df, ds) + self.half)
        return block if part is None else self.part(block, part)

    def copy(self, mine, label, part, to):
        place = self.half * len(LABELS) + PLACE[label]
        ref = self.ref(mine[0], mine[1], part)
        return pltpu.make_async_remote_copy(
            src_ref=ref,
            dst_ref=ref,
            send_sem=self.send.at[place],
            recv_sem=self.recv.at[place],
            device_id={"leaf": to},
            device_id_type=MESH,
        )

    def push(self, mine, label, to):
        copy = self.copy(mine, label, label[2], to)
        copy.start()
        self.sent.append(copy)

    def wait(self, *labels):
        for label in labels:
            self.copy(label[:2], label, label[2], self.device(1, 0)).wait_recv()

    def along_first(self, ahead):
        return self.device(3 if ahead else 1, 0)

    def along_second(self, ahead):
        return self.device(0, 3 if ahead else 1)

    def spread(self, df):
        self.push((df, 0), (df, 1, None), self.along_second(True))
        self.push((df, 0), (df, 3, None), self.along_second(False))

    def relay(self, df):
        self.wait((df, 1, None))
        self.push((df, 1), (df, 2, 0), self.along_second(True))
        self.wait((df, 3, None))
        self.push((df, 3), (df, 2, 1), self.along_second(False))

    def step0(self):
        self.push((0, 0), (1, 0, None), self.along_first(True))
        self.push((0, 0), (3, 0, None), self.along_first(False))
        self.spread(0)

    def step1(self):
        self.wait((1, 0, None))
        self.push((1, 0), (2, 0, 0), self.along_first(True))
        self.spread(1)
        self.wait((3, 0, None))
        self.push((3, 0), (2, 0, 1), self.along_first(False))
        self.spread(3)
        self.relay(0)

    def step2(self):
        self.wait((2, 0, 0), (2, 0, 1))
        self.spread(2)
        self.relay(1)
        self.relay(3)

    def step3(self):
        self.relay(2)

    def step4(self):
        self.wait(*[(df, 2, part) for df in (0, 1, 3, 2) for part in (0, 1)])

    def finish(self):
        for copy in self.sent:
            copy.wait_send()


class Exchange:
    def __init__(self, axis, size, me, block, send, recv):
        self.axis, self.size, self.me, self.block = axis, size, me, block
        self.send, self.recv = send, recv
        self.sent = []

    def copy(self, owner, step, to):
        ref = self.block(owner)
        return pltpu.make_async_remote_copy(
            src_ref=ref,
            dst_ref=ref,
            send_sem=self.send.at[step],
            recv_sem=self.recv.at[step],
            device_id={self.axis: to},
            device_id_type=MESH,
        )

    def start(self):
        for step in range(1, self.size):
            copy = self.copy(self.me, step, lax.rem(self.me + step, self.size))
            copy.start()
            self.sent.append(copy)

    def wait(self):
        for step in range(1, self.size):
            owner = lax.rem(self.me + self.size - step, self.size)
            self.copy(owner, step, owner).wait_recv()

    def finish(self):
        for copy in self.sent:
            copy.wait_send()


def body(
    points_ref,
    right_ref,
    listed_ref,
    count_ref,
    mid_pick_ref,
    top_pick_ref,
    mid_basis_ref,
    top_basis_ref,
    noise_ref,
    solution_ref,
    residual_ref,
    all_points,
    fields0,
    fields1,
    own3,
    coords,
    roots,
    weights,
    tops,
    sums_leaf,
    sums_grp,
    basis,
    basis_high,
    basis_low,
    near_sum,
    image,
    term,
    kept,
    basis_sem,
    points_send,
    points_recv,
    field_send,
    field_recv,
    coords_send,
    coords_recv,
    roots_send,
    roots_recv,
    weights_send,
    weights_recv,
    tops_send,
    tops_recv,
    sums_leaf_send,
    sums_leaf_recv,
    sums_grp_send,
    sums_grp_recv,
):
    me, grp = lax.axis_index("leaf"), lax.axis_index("grp")
    all_fields = (fields0, fields1)

    loads = [
        pltpu.make_async_copy(ref, basis.at[i], basis_sem.at[i])
        for i, ref in enumerate((mid_basis_ref, top_basis_ref))
    ]
    for load in loads:
        load.start()

    barrier = pltpu.get_barrier_semaphore()
    for axis, own, size in (("leaf", me, N_LEAF), ("grp", grp, N_GRP)):
        for step in range(1, size):
            pl.semaphore_signal(
                barrier, inc=1, device_id={axis: lax.rem(own + step, size)}, device_id_type=MESH
            )

    points = points_ref[...]
    right = right_ref[...]
    scale = self_scale(points)
    field = right * scale
    for slot in range(2):
        columns = slice(slot * LEAF, (slot + 1) * LEAF)
        all_points[2 * me + slot] = points[:, columns]
        fields0[2 * me + slot] = field[:, columns]
        own3[slot] = thirds(points[:, columns])

    pl.semaphore_wait(barrier, N_LEAF + N_GRP - 2)

    def gathers(slot_of, part_of, send, recv):
        return [Gather(half, me, slot_of, part_of, send, recv) for half in range(2)]

    point_gathers = gathers(
        lambda leaf: all_points.at[leaf],
        lambda block, part: block.at[pl.ds(16 * part, 16)],
        points_send,
        points_recv,
    )
    field_gathers = [
        gathers(
            lambda leaf, it=it: all_fields[it].at[leaf],
            lambda block, part: block.at[:, pl.ds(512 * part, 512)],
            field_send.at[it],
            field_recv.at[it],
        )
        for it in range(2)
    ]
    first_gathers = [point_gathers[0], point_gathers[1], field_gathers[0][0], field_gathers[0][1]]
    coord_exchange = Exchange(
        "leaf", N_LEAF, me, lambda dev: coords.at[dev], coords_send, coords_recv
    )
    root_exchange = Exchange("grp", N_GRP, grp, lambda g: roots.at[g], roots_send, roots_recv)
    weight_exchange = [
        Exchange(
            "leaf",
            N_LEAF,
            me,
            lambda dev, it=it: weights.at[it, dev],
            weights_send.at[it],
            weights_recv.at[it],
        )
        for it in range(2)
    ]
    top_exchange = [
        Exchange(
            "grp", N_GRP, grp, lambda g, it=it: tops.at[it, g], tops_send.at[it], tops_recv.at[it]
        )
        for it in range(2)
    ]

    def step(gathered, name):
        for gather in gathered:
            getattr(gather, name)()

    def add_block(it, slot, place, rows_of, field16):
        total = None
        for start in range(0, LEAF, CHUNK):
            rows = pl.ds(start, CHUNK)
            if it == 1 and place is not None:
                high, low = kept[place, 0, rows, :], kept[place, 1, rows, :]
            else:
                high, low = kernel_halves(rows_of(rows), own3[slot])
                if place is not None:
                    kept[place, 0, rows, :] = high
                    kept[place, 1, rows, :] = low
            part = applied(field16[:, start : start + CHUNK], high, low)
            total = part if total is None else total + part
        near_sum[slot] += total

    def near_self(it, slot):
        near_sum[slot] = jnp.zeros((2 * TARGETS, LEAF), F32)
        field16 = stacked(all_fields[it][2 * me + slot] * count_ref[slot].astype(F32))
        columns = slot * LEAF
        add_block(
            it,
            slot,
            None,
            lambda rows: points_ref[:, pl.ds(columns + rows.start, CHUNK)],
            field16,
        )

    def near_listed(it, slot, begin, end):
        count = count_ref[slot]

        def run(low_end, high_end, keep):
            def one(k, carried):
                leaf = listed_ref[slot, k]
                active = jnp.where(k < count, 1.0, 0.0).astype(F32)
                field16 = stacked(all_fields[it][leaf] * active)
                place = slot * (SLOTS - 1) + k - 1 if keep else None
                rows_of = lambda rows: all_points[leaf, :, rows]
                add_block(it, slot, place, rows_of, field16)
                return carried

            if low_end < high_end:
                lax.fori_loop(low_end, high_end, one, 0)

        limit = min(max(KEPT - slot * (SLOTS - 1) + 1, 1), SLOTS)
        run(begin, min(end, limit), True)
        run(max(begin, limit), end, False)

    def near(slot):
        return folded(near_sum[slot]) * (scale[:, slot * LEAF : (slot + 1) * LEAF] * LEAF**-0.5)

    def project(value):
        value16 = stacked(value)
        return folded(dot_nt(value16, basis_high[...]) + dot_nt(value16, basis_low[...]))

    def side_by_side(blocks):
        return jnp.concatenate(blocks, axis=1)

    def skeleton_image(coords_of, weights_of, count, columns3):
        total = jnp.zeros((2 * TARGETS, RANK), F32)
        for start in range(0, count, 4):
            rows = side_by_side([coords_of(start + i) for i in range(4)])
            field16 = stacked(side_by_side([weights_of(start + i) for i in range(4)]))
            total = total + applied(field16, *kernel_halves(rows, columns3))
        return folded(total)

    step(first_gathers, "step0")

    def picked(pick, base):
        found = jnp.zeros((FEATURES, RANK), F32)
        for start in range(0, BLOCK, CHUNK):
            rows = lax.broadcasted_iota(jnp.int32, (CHUNK, RANK), 0) + (base + start)
            chosen = jnp.where(rows == pick, 1.0, 0.0).astype(BF16)
            found = found + dot(points[:, start : start + CHUNK], chosen)
        return found.astype(BF16)

    own_mid = picked(mid_pick_ref[...], 0)
    coords[me, 0:FEATURES, :] = own_mid
    coords[me, FEATURES : 2 * FEATURES, :] = picked(top_pick_ref[...], me * BLOCK)
    mid3, mid_scale = thirds(own_mid), self_scale(own_mid)

    step(first_gathers, "step1")
    coord_exchange.start()
    near_self(0, 0)
    step(first_gathers, "step2")

    for load in loads:
        load.wait()
    for i in range(2):
        for start in range(0, RANK, 64):
            high, low = halves(basis[i, start : start + 64, :])
            basis_high[i * RANK + start : i * RANK + start + 64, :] = high
            basis_low[i * RANK + start : i * RANK + start + 64, :] = low

    def send_weights(it, value, sums):
        parts = project(value)
        weights[it, me, 0] = parts[:, :RANK] * mid_scale
        weights[it, me, 1] = parts[:, RANK:]
        weights[it, me, 2] = sums
        weight_exchange[it].start()

    blank = jnp.zeros((TARGETS, RANK), F32)
    send_weights(0, right, blank)
    step(first_gathers, "step3")
    near_self(0, 1)

    coord_exchange.wait()
    own_root = jnp.zeros((FEATURES, RANK), F32)
    for dev in range(N_LEAF):
        own_root = own_root + coords[dev, FEATURES : 2 * FEATURES, :].astype(F32)
    own_root = own_root.astype(BF16)
    roots[grp] = own_root
    root_exchange.start()
    root3, root_scale = thirds(own_root), self_scale(own_root)

    def mid_image(it):
        weight_exchange[it].wait()
        top, sums = weights[it, 0, 1], weights[it, 0, 2]
        for dev in range(1, N_LEAF):
            top = top + weights[it, dev, 1]
            sums = sums + weights[it, dev, 2]
        tops[it, grp, 0] = top * root_scale
        tops[it, grp, 1] = sums
        top_exchange[it].start()
        found = skeleton_image(
            lambda dev: coords[dev, 0:FEATURES, :], lambda dev: weights[it, dev, 0], N_LEAF, mid3
        )
        return found * (mid_scale * RANK**-0.5)

    def expand(it, mid_part):
        top_exchange[it].wait()
        found = skeleton_image(lambda g: roots[g], lambda g: tops[it, g, 0], N_GRP, root3)
        top_part = found * (root_scale * RANK**-0.5)
        image16 = stacked(side_by_side([mid_part, top_part]))
        for start in range(0, BLOCK, CHUNK):
            columns = slice(start, start + CHUNK)
            term[:, columns] = folded(
                applied(image16, basis_high[:, columns], basis_low[:, columns])
            )

    mid_part = mid_image(0)
    step(first_gathers, "step4")
    noise = noise_ref[0]

    def finish_leaf(slot, value):
        columns = slice(slot * LEAF, (slot + 1) * LEAF)
        return noise * value[:, columns] + near(slot) + term[:, columns]

    near_listed(0, 0, 1, SLOTS)
    root_exchange.wait()
    expand(0, mid_part)
    second_gathers = field_gathers[1]

    def send_leaf(slot):
        columns = slice(slot * LEAF, (slot + 1) * LEAF)
        found = finish_leaf(slot, right)
        image[:, columns] = found
        fields1[2 * me + slot] = found * scale[:, columns]
        second_gathers[slot].step0()

    send_leaf(0)
    near_listed(0, 1, 1, 3)
    second_gathers[0].step1()
    near_listed(0, 1, 3, 5)
    second_gathers[0].step2()
    near_listed(0, 1, 5, 7)
    second_gathers[0].step3()
    near_listed(0, 1, 7, 8)
    send_leaf(1)

    lane = lax.broadcasted_iota(jnp.int32, (TARGETS, RANK), 1)

    def summed(value):
        return jnp.sum(value, axis=1, keepdims=True)

    first_image = image[...]
    sums = jnp.where(
        lane == 0,
        summed(right * right),
        jnp.where(lane == 1, summed(right * first_image), summed(first_image * first_image)),
    )
    send_weights(1, first_image, sums)
    second_gathers[1].step1()
    near_self(1, 0)
    second_gathers[1].step2()
    near_self(1, 1)
    second_gathers[1].step3()
    mid_part = mid_image(1)
    step(second_gathers, "step4")
    near_listed(1, 0, 1, SLOTS)
    expand(1, mid_part)
    near_listed(1, 1, 1, SLOTS)

    totals = tops[1, 0, 1]
    for g in range(1, N_GRP):
        totals = totals + tops[1, g, 1]
    norm0, curve0, square0 = totals[:, 0:1], totals[:, 1:2], totals[:, 2:3]
    alpha = norm0 / curve0
    norm1 = norm0 - 2.0 * alpha * curve0 + alpha * alpha * square0
    beta = norm1 / norm0
    second_image = jnp.concatenate(
        [finish_leaf(0, first_image), finish_leaf(1, first_image)], axis=1
    )
    residual = right - alpha * first_image
    direction = residual + beta * right
    image1 = (1.0 + beta) * first_image - alpha * second_image

    sums_leaf[me] = jnp.broadcast_to(summed(direction * image1), (TARGETS, 128))
    leaf_exchange = Exchange(
        "leaf", N_LEAF, me, lambda dev: sums_leaf.at[dev], sums_leaf_send, sums_leaf_recv
    )
    leaf_exchange.start()
    leaf_exchange.wait()
    total = sums_leaf[0]
    for dev in range(1, N_LEAF):
        total = total + sums_leaf[dev]
    sums_grp[grp] = total
    grp_exchange = Exchange(
        "grp", N_GRP, grp, lambda g: sums_grp.at[g], sums_grp_send, sums_grp_recv
    )
    grp_exchange.start()
    grp_exchange.wait()
    total = sums_grp[0]
    for g in range(1, N_GRP):
        total = total + sums_grp[g]
    alpha1 = norm1 / total[:, 0:1]
    solution_ref[...] = alpha * right + alpha1 * direction
    residual_ref[...] = residual - alpha1 * image1

    for sender in (
        *first_gathers,
        *second_gathers,
        coord_exchange,
        root_exchange,
        *weight_exchange,
        *top_exchange,
        leaf_exchange,
        grp_exchange,
    ):
        sender.finish()


def on_device(*operands):
    vmem, smem, anywhere = (
        pl.BlockSpec(memory_space=space) for space in (pltpu.VMEM, pltpu.SMEM, pl.ANY)
    )
    messages = 2 * len(LABELS)
    dma = pltpu.SemaphoreType.DMA
    out = jax.ShapeDtypeStruct((TARGETS, BLOCK), F32)
    return pl.pallas_call(
        body,
        out_shape=(out, out),
        in_specs=[vmem, vmem, smem, smem, vmem, vmem, anywhere, anywhere, smem],
        out_specs=(vmem, vmem),
        scratch_shapes=[
            pltpu.VMEM((2 * N_LEAF, FEATURES, LEAF), BF16),
            pltpu.VMEM((2 * N_LEAF, TARGETS, LEAF), F32),
            pltpu.VMEM((2 * N_LEAF, TARGETS, LEAF), F32),
            pltpu.VMEM((2, 3 * FEATURES, LEAF), BF16),
            pltpu.VMEM((N_LEAF, 2 * FEATURES, RANK), BF16),
            pltpu.VMEM((N_GRP, FEATURES, RANK), BF16),
            pltpu.VMEM((2, N_LEAF, 3, TARGETS, RANK), F32),
            pltpu.VMEM((2, N_GRP, 2, TARGETS, RANK), F32),
            pltpu.VMEM((N_LEAF, TARGETS, 128), F32),
            pltpu.VMEM((N_GRP, TARGETS, 128), F32),
            pltpu.VMEM((2, RANK, BLOCK), F32),
            pltpu.VMEM((2 * RANK, BLOCK), BF16),
            pltpu.VMEM((2 * RANK, BLOCK), BF16),
            pltpu.VMEM((2, 2 * TARGETS, LEAF), F32),
            pltpu.VMEM((TARGETS, BLOCK), F32),
            pltpu.VMEM((TARGETS, BLOCK), F32),
            pltpu.VMEM((KEPT, 2, LEAF, LEAF), BF16),
            dma((2,)),
            dma((messages,)),
            dma((messages,)),
            dma((2, messages)),
            dma((2, messages)),
            dma((N_LEAF,)),
            dma((N_LEAF,)),
            dma((N_GRP,)),
            dma((N_GRP,)),
            dma((2, N_LEAF)),
            dma((2, N_LEAF)),
            dma((2, N_GRP)),
            dma((2, N_GRP)),
            dma((N_LEAF,)),
            dma((N_LEAF,)),
            dma((N_GRP,)),
            dma((N_GRP,)),
        ],
        compiler_params=pltpu.CompilerParams(
            collective_id=0, has_side_effects=True, vmem_limit_bytes=62 * 2**20
        ),
    )(*operands)


def solution(mesh):
    placed = (
        P(None, ("grp", "leaf")),
        P(None, ("grp", "leaf")),
        P(("grp", "leaf"), None),
        P(("grp", "leaf")),
        P(("grp", "leaf"), None),
        P("grp", None),
        P(None, ("grp", "leaf")),
        P(None, ("grp", "leaf")),
        P(),
    )
    return jax.shard_map(
        on_device,
        mesh=mesh,
        in_specs=placed,
        out_specs=(P(None, ("grp", "leaf")), P(None, ("grp", "leaf"))),
        check_vma=False,
    )
```

time: 737 us -> 110 us (0.15); the launches traced: 726 us -> 110 us
  blocking collectives: 378 us -> 0 us
  matrix products: 193 us -> 0 us
  Pallas kernels: 0 us -> 105 us
  loops' own time: 72.6 us -> 0 us
  other arithmetic: 45.8 us -> 0 us
  local copies, waits for them, and re-layouts: 18.6 us -> 2.95 us
  between operations: 16.3 us -> 1.29 us
    psum x5 -> x0, blocking collectives: 262 us -> none  [the longest x2 127 us: residual_norm(): return lax.psum(jnp.sum(residual * residual, axis=1), ('grp', 'leaf'))]
    dot_general x76 -> x0, matrix products: 193 us -> none  [the longest x40 130 us: exact_dot(): jnp.dot(left_cols, right_cols, precision=lax.Precision.HIGHEST, preferred...]
    all_gather x6 -> x0, blocking collectives: 116 us -> none  [the longest x2 41.3 us: on_device(): top_weights = lax.all_gather(summed, 'grp', axis=1, tiled=True)]
    pallas_call x0 -> x1, Pallas kernels: none -> 105 us  [on_device(): pl.pallas_call(body, out_shape=(out, out), in_specs=[vmem, vmem, smem, sm...]
    another operation x32 -> x0, loops' own time: 72.6 us -> none  [the longest x28 52.7 us: slot_step(): lax.cond(slot_index < listed, compute, lambda current: current, carried)]
    reduce_sum x34 -> x0, other arithmetic: 27.3 us -> none  [the longest x30 25.2 us: kernel(): right_sq = jnp.sum(jnp.square(right_cols.astype(jnp.float32)), axis=0)]
    mul x28 -> x0, other arithmetic: 16.9 us -> none  [compute(): partner * LEAF]
    while x1 -> x0, local copies, waits for them, and re-layouts: 7.93 us -> none  [near_rows(): running = lax.fori_loop(1, NEIGHBOURS, slot_step, running)]
  transfers between devices with their start and end apart: 3 -> 0, of which waited for: 0 -> 0; matrix products, arithmetic and copies ran while one was open for 8% -> 0% of each run, Pallas kernels for 0% -> 0%
where the time goes in v1:
time: 110 us
  Pallas kernels  105 us (95%)
  local copies, waits for them, and re-layouts  2.95 us (3%)
  between operations  1.29 us (1%)
    pallas_call x1, Pallas kernels, on_device(): pl.pallas_call(body, out_shape=(out, out), in_specs=[vmem, vmem, smem, sm...  105 us
    unnamed x2, local copies, waits for them, and re-layouts  2.95 us

profile of v1, /device:TPU:1, one launch (start us, length us, event | category | flops | bytes accessed | tf_op | source)
XLA Modules:
  0.0 109.6 jit_solution(6566785685654876843)
XLA Ops:
  1.3 105.4 %shard_map.104 = (f32[8,2048]{1,0:T(8,128)}, f32[8,2048]{1,0:T(8,128)}) custom-call(bf16[32,2048]{1,0:T(8,128)(2,1)} %points_ref.1, f32[8,2048]{1,0:T(8,128)} %right_ref.1, s32[2,8]{1,0:T(2,128)} %listed_ref.1, s32[2]{0:T(128)} %count_ref.1, s32[1,256]{1,0:T(1,128)} %mid_pick_ref.1, s32[1,256]{1,0:T(1,128)} %top_pick_ref.1, f32[256,2048]{1,0:T(8,128)} %mid_basis_ref.1, ...), custom_call_target="tpu_custom_call" | custom-call | tf_op jit(solution)/shard_map/pallas_call | solution.py:570
  106.7 1.5 %copy.14 = f32[8,2048]{1,0:T(8,128)} copy(f32[8,2048]{1,0:T(8,128)} %get-tuple-element.4) | data formatting | bytes 131072
  108.2 1.5 %copy.15 = f32[8,2048]{1,0:T(8,128)} copy(f32[8,2048]{1,0:T(8,128)} %get-tuple-element.5) | data formatting | bytes 131072

commit v2 on v1

--- a/solution.py
+++ b/solution.py
@@ -17,7 +17,8 @@
 N_GRP = 8
 BLOCK = 2 * LEAF
 CHUNK = 512
-KEPT = 8
+KEPT = 10
+PIECES = ((0, 0, LEAF), (1, 0, LEAF // 2), (1, LEAF // 2, LEAF // 2))
 MESH = pl.DeviceIdType.MESH
 F32 = jnp.float32
 BF16 = jnp.bfloat16
@@ -94,7 +95,7 @@
         return f * SIDE + s if self.half == 0 else s * SIDE + f
 
     def ref(self, df, ds, part):
-        block = self.slot(2 * self.device(df, ds) + self.half)
+        block = self.slot(self.device(df, ds))
         return block if part is None else self.part(block, part)
 
     def copy(self, mine, label, part, to):
@@ -214,7 +215,8 @@
     fields0,
     fields1,
     own3,
-    coords,
+    mid_coords,
+    top_coords,
     roots,
     weights,
     tops,
@@ -232,6 +234,8 @@
     points_recv,
     field_send,
     field_recv,
+    image_send,
+    image_recv,
     coords_send,
     coords_recv,
     roots_send,
@@ -275,34 +279,48 @@
     pl.semaphore_wait(barrier, N_LEAF + N_GRP - 2)
 
     def gathers(slot_of, part_of, send, recv):
-        return [Gather(half, me, slot_of, part_of, send, recv) for half in range(2)]
+        return [
+            Gather(half, me, lambda dev, half=half: slot_of(half, dev), part_of, send, recv)
+            for half in range(2)
+        ]
 
     point_gathers = gathers(
-        lambda leaf: all_points.at[leaf],
+        lambda half, dev: all_points.at[2 * dev + half],
         lambda block, part: block.at[pl.ds(16 * part, 16)],
         points_send,
         points_recv,
     )
-    field_gathers = [
-        gathers(
-            lambda leaf, it=it: all_fields[it].at[leaf],
-            lambda block, part: block.at[:, pl.ds(512 * part, 512)],
-            field_send.at[it],
-            field_recv.at[it],
+    first_field_gathers = gathers(
+        lambda half, dev: fields0.at[2 * dev + half],
+        lambda block, part: block.at[:, pl.ds(512 * part, 512)],
+        field_send,
+        field_recv,
+    )
+    coord_gathers = gathers(
+        lambda half, dev: (mid_coords, top_coords)[half].at[dev],
+        lambda block, part: block.at[pl.ds(16 * part, 16)],
+        coords_send,
+        coords_recv,
+    )
+    first_gathers = [*point_gathers, *first_field_gathers]
+    image_exchange = [
+        Exchange(
+            "leaf",
+            N_LEAF,
+            me,
+            lambda dev, piece=piece: fields1.at[2 * dev + piece[0], :, pl.ds(piece[1], piece[2])],
+            image_send.at[i],
+            image_recv.at[i],
         )
-        for it in range(2)
+        for i, piece in enumerate(PIECES)
     ]
-    first_gathers = [point_gathers[0], point_gathers[1], field_gathers[0][0], field_gathers[0][1]]
-    coord_exchange = Exchange(
-        "leaf", N_LEAF, me, lambda dev: coords.at[dev], coords_send, coords_recv
-    )
     root_exchange = Exchange("grp", N_GRP, grp, lambda g: roots.at[g], roots_send, roots_recv)
     weight_exchange = [
         Exchange(
             "leaf",
             N_LEAF,
             me,
-            lambda dev, it=it: weights.at[it, dev],
+            lambda dev, it=it: weights.at[it, dev, pl.ds(0, 2 + it)],
             weights_send.at[it],
             weights_recv.at[it],
         )
@@ -310,7 +328,12 @@
     ]
     top_exchange = [
         Exchange(
-            "grp", N_GRP, grp, lambda g, it=it: tops.at[it, g], tops_send.at[it], tops_recv.at[it]
+            "grp",
+            N_GRP,
+            grp,
+            lambda g, it=it: tops.at[it, g, pl.ds(0, 1 + it)],
+            tops_send.at[it],
+            tops_recv.at[it],
         )
         for it in range(2)
     ]
@@ -319,34 +342,31 @@
         for gather in gathered:
             getattr(gather, name)()
 
-    def add_block(it, slot, place, rows_of, field16):
+    def add_block(it, slot, place, rows_of, field16, start, width):
+        columns = pl.ds(start, width)
+        height = CHUNK * LEAF // width
         total = None
-        for start in range(0, LEAF, CHUNK):
-            rows = pl.ds(start, CHUNK)
+        for first in range(0, LEAF, height):
+            rows = pl.ds(first, height)
             if it == 1 and place is not None:
-                high, low = kept[place, 0, rows, :], kept[place, 1, rows, :]
+                high, low = kept[place, 0, rows, columns], kept[place, 1, rows, columns]
             else:
-                high, low = kernel_halves(rows_of(rows), own3[slot])
+                high, low = kernel_halves(rows_of(rows), own3[slot, :, columns])
                 if place is not None:
-                    kept[place, 0, rows, :] = high
-                    kept[place, 1, rows, :] = low
-            part = applied(field16[:, start : start + CHUNK], high, low)
+                    kept[place, 0, rows, columns] = high
+                    kept[place, 1, rows, columns] = low
+            part = applied(field16[:, first : first + height], high, low)
             total = part if total is None else total + part
-        near_sum[slot] += total
+        near_sum[slot, :, columns] += total
 
     def near_self(it, slot):
         near_sum[slot] = jnp.zeros((2 * TARGETS, LEAF), F32)
         field16 = stacked(all_fields[it][2 * me + slot] * count_ref[slot].astype(F32))
-        columns = slot * LEAF
-        add_block(
-            it,
-            slot,
-            None,
-            lambda rows: points_ref[:, pl.ds(columns + rows.start, CHUNK)],
-            field16,
-        )
-
-    def near_listed(it, slot, begin, end):
+        base = slot * LEAF
+        rows_of = lambda rows: points_ref[:, pl.ds(base + rows.start, rows.size)]
+        add_block(it, slot, None, rows_of, field16, 0, LEAF)
+
+    def near_listed(it, slot, begin=1, end=SLOTS, start=0, width=LEAF):
         count = count_ref[slot]
 
         def run(low_end, high_end, keep):
@@ -356,7 +376,7 @@
                 field16 = stacked(all_fields[it][leaf] * active)
                 place = slot * (SLOTS - 1) + k - 1 if keep else None
                 rows_of = lambda rows: all_points[leaf, :, rows]
-                add_block(it, slot, place, rows_of, field16)
+                add_block(it, slot, place, rows_of, field16, start, width)
                 return carried
 
             if low_end < high_end:
@@ -366,8 +386,10 @@
         run(begin, min(end, limit), True)
         run(max(begin, limit), end, False)
 
-    def near(slot):
-        return folded(near_sum[slot]) * (scale[:, slot * LEAF : (slot + 1) * LEAF] * LEAF**-0.5)
+    def near(slot, start, width):
+        columns = pl.ds(start, width)
+        base = slot * LEAF + start
+        return folded(near_sum[slot, :, columns]) * (scale[:, base : base + width] * LEAF**-0.5)
 
     def project(value):
         value16 = stacked(value)
@@ -395,14 +417,15 @@
         return found.astype(BF16)
 
     own_mid = picked(mid_pick_ref[...], 0)
-    coords[me, 0:FEATURES, :] = own_mid
-    coords[me, FEATURES : 2 * FEATURES, :] = picked(top_pick_ref[...], me * BLOCK)
+    mid_coords[me] = own_mid
+    top_coords[me] = picked(top_pick_ref[...], me * BLOCK)
     mid3, mid_scale = thirds(own_mid), self_scale(own_mid)
 
+    step(coord_gathers, "step0")
     step(first_gathers, "step1")
-    coord_exchange.start()
     near_self(0, 0)
     step(first_gathers, "step2")
+    step(coord_gathers, "step1")
 
     for load in loads:
         load.wait()
@@ -416,34 +439,31 @@
         parts = project(value)
         weights[it, me, 0] = parts[:, :RANK] * mid_scale
         weights[it, me, 1] = parts[:, RANK:]
-        weights[it, me, 2] = sums
+        if sums is not None:
+            weights[it, me, 2] = sums
         weight_exchange[it].start()
 
-    blank = jnp.zeros((TARGETS, RANK), F32)
-    send_weights(0, right, blank)
     step(first_gathers, "step3")
     near_self(0, 1)
-
-    coord_exchange.wait()
-    own_root = jnp.zeros((FEATURES, RANK), F32)
-    for dev in range(N_LEAF):
-        own_root = own_root + coords[dev, FEATURES : 2 * FEATURES, :].astype(F32)
-    own_root = own_root.astype(BF16)
-    roots[grp] = own_root
-    root_exchange.start()
-    root3, root_scale = thirds(own_root), self_scale(own_root)
+    step(coord_gathers, "step2")
+    send_weights(0, right, None)
+    step(coord_gathers, "step3")
+    step(first_gathers, "step4")
 
     def mid_image(it):
         weight_exchange[it].wait()
-        top, sums = weights[it, 0, 1], weights[it, 0, 2]
+        top = weights[it, 0, 1]
         for dev in range(1, N_LEAF):
             top = top + weights[it, dev, 1]
-            sums = sums + weights[it, dev, 2]
         tops[it, grp, 0] = top * root_scale
-        tops[it, grp, 1] = sums
+        if it == 1:
+            sums = weights[it, 0, 2]
+            for dev in range(1, N_LEAF):
+                sums = sums + weights[it, dev, 2]
+            tops[it, grp, 1] = sums
         top_exchange[it].start()
         found = skeleton_image(
-            lambda dev: coords[dev, 0:FEATURES, :], lambda dev: weights[it, dev, 0], N_LEAF, mid3
+            lambda dev: mid_coords[dev], lambda dev: weights[it, dev, 0], N_LEAF, mid3
         )
         return found * (mid_scale * RANK**-0.5)
 
@@ -458,35 +478,35 @@
                 applied(image16, basis_high[:, columns], basis_low[:, columns])
             )
 
+    noise = noise_ref[0]
+
+    def finished(value, slot, start, width):
+        base = slot * LEAF + start
+        columns = slice(base, base + width)
+        return noise * value[:, columns] + near(slot, start, width) + term[:, columns]
+
+    near_listed(0, 0, 1, 4)
+    step(coord_gathers, "step4")
+    own_root = jnp.zeros((FEATURES, RANK), F32)
+    for dev in range(N_LEAF):
+        own_root = own_root + top_coords[dev].astype(F32)
+    own_root = own_root.astype(BF16)
+    roots[grp] = own_root
+    root_exchange.start()
+    root3, root_scale = thirds(own_root), self_scale(own_root)
     mid_part = mid_image(0)
-    step(first_gathers, "step4")
-    noise = noise_ref[0]
-
-    def finish_leaf(slot, value):
-        columns = slice(slot * LEAF, (slot + 1) * LEAF)
-        return noise * value[:, columns] + near(slot) + term[:, columns]
-
-    near_listed(0, 0, 1, SLOTS)
+    near_listed(0, 0, 4, 8)
     root_exchange.wait()
     expand(0, mid_part)
-    second_gathers = field_gathers[1]
-
-    def send_leaf(slot):
-        columns = slice(slot * LEAF, (slot + 1) * LEAF)
-        found = finish_leaf(slot, right)
-        image[:, columns] = found
-        fields1[2 * me + slot] = found * scale[:, columns]
-        second_gathers[slot].step0()
-
-    send_leaf(0)
-    near_listed(0, 1, 1, 3)
-    second_gathers[0].step1()
-    near_listed(0, 1, 3, 5)
-    second_gathers[0].step2()
-    near_listed(0, 1, 5, 7)
-    second_gathers[0].step3()
-    near_listed(0, 1, 7, 8)
-    send_leaf(1)
+
+    for exchange, (slot, start, width) in zip(image_exchange, PIECES, strict=True):
+        if slot == 1:
+            near_listed(0, slot, start=start, width=width)
+        found = finished(right, slot, start, width)
+        base = slot * LEAF + start
+        image[:, base : base + width] = found
+        fields1[2 * me + slot, :, start : start + width] = found * scale[:, base : base + width]
+        exchange.start()
 
     lane = lax.broadcasted_iota(jnp.int32, (TARGETS, RANK), 1)
 
@@ -500,16 +520,14 @@
         jnp.where(lane == 1, summed(right * first_image), summed(first_image * first_image)),
     )
     send_weights(1, first_image, sums)
-    second_gathers[1].step1()
     near_self(1, 0)
-    second_gathers[1].step2()
     near_self(1, 1)
-    second_gathers[1].step3()
+    for exchange in image_exchange:
+        exchange.wait()
+    near_listed(1, 0)
     mid_part = mid_image(1)
-    step(second_gathers, "step4")
-    near_listed(1, 0, 1, SLOTS)
+    near_listed(1, 1)
     expand(1, mid_part)
-    near_listed(1, 1, 1, SLOTS)
 
     totals = tops[1, 0, 1]
     for g in range(1, N_GRP):
@@ -519,7 +537,7 @@
     norm1 = norm0 - 2.0 * alpha * curve0 + alpha * alpha * square0
     beta = norm1 / norm0
     second_image = jnp.concatenate(
-        [finish_leaf(0, first_image), finish_leaf(1, first_image)], axis=1
+        [finished(first_image, slot, 0, LEAF) for slot in range(2)], axis=1
     )
     residual = right - alpha * first_image
     direction = residual + beta * right
@@ -549,8 +567,8 @@
 
     for sender in (
         *first_gathers,
-        *second_gathers,
-        coord_exchange,
+        *coord_gathers,
+        *image_exchange,
         root_exchange,
         *weight_exchange,
         *top_exchange,
@@ -577,7 +595,8 @@
             pltpu.VMEM((2 * N_LEAF, TARGETS, LEAF), F32),
             pltpu.VMEM((2 * N_LEAF, TARGETS, LEAF), F32),
             pltpu.VMEM((2, 3 * FEATURES, LEAF), BF16),
-            pltpu.VMEM((N_LEAF, 2 * FEATURES, RANK), BF16),
+            pltpu.VMEM((N_LEAF, FEATURES, RANK), BF16),
+            pltpu.VMEM((N_LEAF, FEATURES, RANK), BF16),
             pltpu.VMEM((N_GRP, FEATURES, RANK), BF16),
             pltpu.VMEM((2, N_LEAF, 3, TARGETS, RANK), F32),
             pltpu.VMEM((2, N_GRP, 2, TARGETS, RANK), F32),
@@ -593,10 +612,12 @@
             dma((2,)),
             dma((messages,)),
             dma((messages,)),
-            dma((2, messages)),
-            dma((2, messages)),
-            dma((N_LEAF,)),
-            dma((N_LEAF,)),
+            dma((messages,)),
+            dma((messages,)),
+            dma((len(PIECES), N_LEAF)),
+            dma((len(PIECES), N_LEAF)),
+            dma((messages,)),
+            dma((messages,)),
             dma((N_GRP,)),
             dma((N_GRP,)),
             dma((2, N_LEAF)),

time: 110 us -> 98 us (0.89)
  Pallas kernels: 105 us -> 93.6 us
    pallas_call x1, Pallas kernels: 105 us -> 93.6 us  [on_device(): pl.pallas_call(body, out_shape=(out, out), in_specs=[vmem, vmem, smem, sm...]
where the time goes in v2:
time: 98 us; the launch traced here: 97.8 us
  Pallas kernels  93.6 us (96%)
  local copies, waits for them, and re-layouts  2.95 us (3%)
  between operations  1.29 us (1%)
    pallas_call x1, Pallas kernels, on_device(): pl.pallas_call(body, out_shape=(out, out), in_specs=[vmem, vmem, smem, sm...  93.6 us
    unnamed x2, local copies, waits for them, and re-layouts  2.95 us

profile of v2, /device:TPU:1, one launch (start us, length us, event | category | flops | bytes accessed | tf_op | source)
XLA Modules:
  0.0 97.8 jit_solution(2314720048749281853)
XLA Ops:
  1.3 93.6 %shard_map.104 = (f32[8,2048]{1,0:T(8,128)}, f32[8,2048]{1,0:T(8,128)}) custom-call(bf16[32,2048]{1,0:T(8,128)(2,1)} %points_ref.1, f32[8,2048]{1,0:T(8,128)} %right_ref.1, s32[2,8]{1,0:T(2,128)} %listed_ref.1, s32[2]{0:T(128)} %count_ref.1, s32[1,256]{1,0:T(1,128)} %mid_pick_ref.1, s32[1,256]{1,0:T(1,128)} %top_pick_ref.1, f32[256,2048]{1,0:T(8,128)} %mid_basis_ref.1, ...), custom_call_target="tpu_custom_call" | custom-call | tf_op jit(solution)/shard_map/pallas_call | solution.py:588
  94.9 1.5 %copy.14 = f32[8,2048]{1,0:T(8,128)} copy(f32[8,2048]{1,0:T(8,128)} %get-tuple-element.4) | data formatting | bytes 131072
  96.3 1.5 %copy.15 = f32[8,2048]{1,0:T(8,128)} copy(f32[8,2048]{1,0:T(8,128)} %get-tuple-element.5) | data formatting | bytes 131072

commit v3 on v2

--- a/solution.py
+++ b/solution.py
@@ -135,30 +135,38 @@
         self.wait((df, 3, None))
         self.push((df, 3), (df, 2, 1), self.along_second(False))
 
-    def step0(self):
+    def own_first(self):
         self.push((0, 0), (1, 0, None), self.along_first(True))
         self.push((0, 0), (3, 0, None), self.along_first(False))
+
+    def own_second(self):
         self.spread(0)
 
-    def step1(self):
+    def relay_first(self):
         self.wait((1, 0, None))
         self.push((1, 0), (2, 0, 0), self.along_first(True))
-        self.spread(1)
         self.wait((3, 0, None))
         self.push((3, 0), (2, 0, 1), self.along_first(False))
+
+    def spread_near(self):
+        self.spread(1)
         self.spread(3)
-        self.relay(0)
-
-    def step2(self):
+
+    def spread_far(self):
         self.wait((2, 0, 0), (2, 0, 1))
         self.spread(2)
+
+    def relay_own(self):
+        self.relay(0)
+
+    def relay_near(self):
         self.relay(1)
         self.relay(3)
 
-    def step3(self):
+    def relay_far(self):
         self.relay(2)
 
-    def step4(self):
+    def arrive(self):
         self.wait(*[(df, 2, part) for df in (0, 1, 3, 2) for part in (0, 1)])
 
     def finish(self):
@@ -211,6 +219,9 @@
     noise_ref,
     solution_ref,
     residual_ref,
+    direction_ref,
+    image_ref,
+    step_ref,
     all_points,
     fields0,
     fields1,
@@ -260,11 +271,12 @@
         load.start()
 
     barrier = pltpu.get_barrier_semaphore()
-    for axis, own, size in (("leaf", me, N_LEAF), ("grp", grp, N_GRP)):
-        for step in range(1, size):
-            pl.semaphore_signal(
-                barrier, inc=1, device_id={axis: lax.rem(own + step, size)}, device_id_type=MESH
-            )
+    x, z = lax.div(me, SIDE), lax.rem(me, SIDE)
+    beside = [{"leaf": lax.rem(x + step, SIDE) * SIDE + z} for step in (1, 3)]
+    beside += [{"leaf": x * SIDE + lax.rem(z + step, SIDE)} for step in (1, 3)]
+    beside += [{"grp": lax.rem(grp + step, N_GRP)} for step in range(1, N_GRP)]
+    for device in beside:
+        pl.semaphore_signal(barrier, inc=1, device_id=device, device_id_type=MESH)
 
     points = points_ref[...]
     right = right_ref[...]
@@ -276,7 +288,7 @@
         fields0[2 * me + slot] = field[:, columns]
         own3[slot] = thirds(points[:, columns])
 
-    pl.semaphore_wait(barrier, N_LEAF + N_GRP - 2)
+    pl.semaphore_wait(barrier, len(beside))
 
     def gathers(slot_of, part_of, send, recv):
         return [
@@ -338,17 +350,25 @@
         for it in range(2)
     ]
 
-    def step(gathered, name):
-        for gather in gathered:
-            getattr(gather, name)()
-
-    def add_block(it, slot, place, rows_of, field16, start, width):
+    def step(gathered, *names):
+        for name in names:
+            for gather in gathered:
+                getattr(gather, name)()
+
+    def make_block(place, rows_of, slot):
+        for first in range(0, LEAF, CHUNK):
+            rows = pl.ds(first, CHUNK)
+            high, low = kernel_halves(rows_of(rows), own3[slot])
+            kept[place, 0, rows, :] = high
+            kept[place, 1, rows, :] = low
+
+    def add_block(ready, slot, place, rows_of, field16, start, width):
         columns = pl.ds(start, width)
         height = CHUNK * LEAF // width
         total = None
         for first in range(0, LEAF, height):
             rows = pl.ds(first, height)
-            if it == 1 and place is not None:
+            if ready and place is not None:
                 high, low = kept[place, 0, rows, columns], kept[place, 1, rows, columns]
             else:
                 high, low = kernel_halves(rows_of(rows), own3[slot, :, columns])
@@ -364,9 +384,9 @@
         field16 = stacked(all_fields[it][2 * me + slot] * count_ref[slot].astype(F32))
         base = slot * LEAF
         rows_of = lambda rows: points_ref[:, pl.ds(base + rows.start, rows.size)]
-        add_block(it, slot, None, rows_of, field16, 0, LEAF)
-
-    def near_listed(it, slot, begin=1, end=SLOTS, start=0, width=LEAF):
+        add_block(False, slot, None, rows_of, field16, 0, LEAF)
+
+    def near_listed(it, slot, begin=1, end=SLOTS, start=0, width=LEAF, ready=True):
         count = count_ref[slot]
 
         def run(low_end, high_end, keep):
@@ -376,7 +396,7 @@
                 field16 = stacked(all_fields[it][leaf] * active)
                 place = slot * (SLOTS - 1) + k - 1 if keep else None
                 rows_of = lambda rows: all_points[leaf, :, rows]
-                add_block(it, slot, place, rows_of, field16, start, width)
+                add_block(ready, slot, place, rows_of, field16, start, width)
                 return carried
 
             if low_end < high_end:
@@ -385,6 +405,14 @@
         limit = min(max(KEPT - slot * (SLOTS - 1) + 1, 1), SLOTS)
         run(begin, min(end, limit), True)
         run(max(begin, limit), end, False)
+
+    def make_listed(slot):
+        def one(k, carried):
+            leaf = listed_ref[slot, k]
+            make_block(slot * (SLOTS - 1) + k - 1, lambda rows: all_points[leaf, :, rows], slot)
+            return carried
+
+        lax.fori_loop(1, SLOTS, one, 0)
 
     def near(slot, start, width):
         columns = pl.ds(start, width)
@@ -406,7 +434,7 @@
             total = total + applied(field16, *kernel_halves(rows, columns3))
         return folded(total)
 
-    step(first_gathers, "step0")
+    step(first_gathers, "own_first", "own_second")
 
     def picked(pick, base):
         found = jnp.zeros((FEATURES, RANK), F32)
@@ -421,11 +449,10 @@
     top_coords[me] = picked(top_pick_ref[...], me * BLOCK)
     mid3, mid_scale = thirds(own_mid), self_scale(own_mid)
 
-    step(coord_gathers, "step0")
-    step(first_gathers, "step1")
+    step(first_gathers, "relay_first", "spread_near")
+    step(coord_gathers, "own_first", "own_second")
     near_self(0, 0)
-    step(first_gathers, "step2")
-    step(coord_gathers, "step1")
+    step(first_gathers, "spread_far", "relay_own", "relay_near")
 
     for load in loads:
         load.wait()
@@ -443,12 +470,15 @@
             weights[it, me, 2] = sums
         weight_exchange[it].start()
 
-    step(first_gathers, "step3")
+    step(first_gathers, "relay_far")
+    step(coord_gathers, "relay_first", "spread_near")
     near_self(0, 1)
-    step(coord_gathers, "step2")
+    step(point_gathers, "arrive")
     send_weights(0, right, None)
-    step(coord_gathers, "step3")
-    step(first_gathers, "step4")
+    step(coord_gathers, "spread_far", "relay_own", "relay_near")
+    make_listed(0)
+    step(first_field_gathers, "arrive")
+    step(coord_gathers, "relay_far")
 
     def mid_image(it):
         weight_exchange[it].wait()
@@ -486,7 +516,7 @@
         return noise * value[:, columns] + near(slot, start, width) + term[:, columns]
 
     near_listed(0, 0, 1, 4)
-    step(coord_gathers, "step4")
+    step(coord_gathers, "arrive")
     own_root = jnp.zeros((FEATURES, RANK), F32)
     for dev in range(N_LEAF):
         own_root = own_root + top_coords[dev].astype(F32)
@@ -501,7 +531,7 @@
 
     for exchange, (slot, start, width) in zip(image_exchange, PIECES, strict=True):
         if slot == 1:
-            near_listed(0, slot, start=start, width=width)
+            near_listed(0, slot, start=start, width=width, ready=False)
         found = finished(right, slot, start, width)
         base = slot * LEAF + start
         image[:, base : base + width] = found
@@ -542,6 +572,10 @@
     residual = right - alpha * first_image
     direction = residual + beta * right
     image1 = (1.0 + beta) * first_image - alpha * second_image
+    solution_ref[...] = alpha * right
+    residual_ref[...] = residual
+    direction_ref[...] = direction
+    image_ref[...] = image1
 
     sums_leaf[me] = jnp.broadcast_to(summed(direction * image1), (TARGETS, 128))
     leaf_exchange = Exchange(
@@ -561,9 +595,7 @@
     total = sums_grp[0]
     for g in range(1, N_GRP):
         total = total + sums_grp[g]
-    alpha1 = norm1 / total[:, 0:1]
-    solution_ref[...] = alpha * right + alpha1 * direction
-    residual_ref[...] = residual - alpha1 * image1
+    step_ref[...] = jnp.broadcast_to(norm1 / total[:, 0:1], (TARGETS, BLOCK))
 
     for sender in (
         *first_gathers,
@@ -585,11 +617,11 @@
     messages = 2 * len(LABELS)
     dma = pltpu.SemaphoreType.DMA
     out = jax.ShapeDtypeStruct((TARGETS, BLOCK), F32)
-    return pl.pallas_call(
+    solution1, residual1, direction, image1, step = pl.pallas_call(
         body,
-        out_shape=(out, out),
+        out_shape=(out,) * 5,
         in_specs=[vmem, vmem, smem, smem, vmem, vmem, anywhere, anywhere, smem],
-        out_specs=(vmem, vmem),
+        out_specs=(vmem,) * 5,
         scratch_shapes=[
             pltpu.VMEM((2 * N_LEAF, FEATURES, LEAF), BF16),
             pltpu.VMEM((2 * N_LEAF, TARGETS, LEAF), F32),
@@ -633,6 +665,7 @@
             collective_id=0, has_side_effects=True, vmem_limit_bytes=62 * 2**20
         ),
     )(*operands)
+    return solution1 + step * direction, residual1 - step * image1
 
 
 def solution(mesh):

time: 98 us -> 97.2 us (level)
  local copies, waits for them, and re-layouts: 2.95 us -> 0 us
  other arithmetic: 0 us -> 1.63 us
    unnamed x2 -> x0, local copies, waits for them, and re-layouts: 2.95 us -> none
    sub x0 -> x1, other arithmetic: none -> 1.63 us  [on_device(): return (solution1 + step * direction, residual1 - step * image1)]
where the time goes in v3:
time: 97.2 us; the launch traced here: 97 us
  Pallas kernels  94.1 us (97%)
  other arithmetic  1.63 us (2%)
  between operations  1.29 us (1%)
    pallas_call x1, Pallas kernels, on_device(): pl.pallas_call(body, out_shape=(out,) * 5, in_specs=[vmem, vmem, smem, sm...  94.1 us

profile of v3, /device:TPU:1, one launch (start us, length us, event | category | flops | bytes accessed | tf_op | source)
XLA Modules:
  0.0 97.0 jit_solution(813537826035629846)
XLA Ops:
  1.3 94.1 %shard_map.104 = (f32[8,2048]{1,0:T(8,128)}, f32[8,2048]{1,0:T(8,128)}, f32[8,2048]{1,0:T(8,128)}, f32[8,2048]{1,0:T(8,128)}, f32[8,2048]{1,0:T(8,128)}) custom-call(bf16[32,2048]{1,0:T(8,128)(2,1)} %points_ref.1, f32[8,2048]{1,0:T(8,128)} %right_ref.1, s32[2,8]{1,0:T(2,128)} %listed_ref.1, s32[2]{0:T(128)} %count_ref.1, s32[1,256]{1,0:T(1,128)} %mid_pick_ref.1, ...), custom_call_target="tpu_custom_call" | custom-call | tf_op jit(solution)/shard_map/pallas_call | solution.py:620
  95.4 1.6 %multiply_subtract_fusion = (f32[8,2048]{1,0:T(8,128)}, f32[8,2048]{1,0:T(8,128)}) fusion(f32[8,2048]{1,0:T(8,128)} %get-tuple-element.10, f32[8,2048]{1,0:T(8,128)} %get-tuple-element.8, f32[8,2048]{1,0:T(8,128)} %get-tuple-element.11, f32[8,2048]{1,0:T(8,128)} %get-tuple-element.7, f32[8,2048]{1,0:T(8,128)} %get-tuple-element.9), kind=kLoop, calls=%fused_computation | loop fusion | flops 65536 | bytes 458752 | tf_op jit(solution)/shard_map/sub | solution.py:668
